TPU v7x, 32 devices: a whole 2x2x4 slice. The times are simulated.
32 devices in a mesh: tm: 8 (over z, y), space: 4 (over x, core).
Axes of the slice: x: 2, y: 2, z: 4, core: 2. Of those that a mesh axis runs over, the one named last changes fastest.
Arguments:
- snapshots: bfloat16 [4096, 3, 4096], P('tm', None, 'space'), may hold values from -6 to 6
- cell_weights: float32 [4096], P('space'), may hold values from 0.25 to 4
- triads: int32 [64, 3], replicated, may hold values from 0 to 127, as said below
- owner_slots: int32 [8, 16], replicated, may hold values from -1 to 63, as said below
Outputs:
- bispectra: float32 [128, 512], P(('tm', 'space'))
Inputs may be any that keep to these rules, and one draw needn't show every extreme that they name: `triads`: every row is (k, l, k + l); all three entries are below 128. `owner_slots`: every triad index stands in exactly one slot of the table; in each row the used slots come first and the others hold -1; some owner fills all 16 slots.
All inputs are finite; a program needn't handle non-finite values.
Results may differ from a plain program's by a relative error of at most 0.0076.
Values may be sent and summed in bfloat16 or wider, within the bound.
A program may use at most 64 MiB of HBM per device.

v0:
```python
import math
import jax
import jax.numpy as jnp
from jax import lax
from jax.sharding import PartitionSpec as P

NB = 16
NT = 256
K = 128


def spectral_table():
    sample = jnp.arange(NT, dtype=jnp.int32)
    freq_bins = jnp.arange(K, dtype=jnp.int32)
    phase_idx = freq_bins[:, None] * sample[None, :] % NT
    angles = 2.0 * math.pi / NT * phase_idx.astype(jnp.float32)
    window = 0.5 - 0.5 * jnp.cos(2.0 * math.pi / NT * sample.astype(jnp.float32))
    norm_scale = math.sqrt(8.0 / (3.0 * NT))
    real_rows = norm_scale * window[None, :] * jnp.cos(angles)
    imag_rows = -norm_scale * window[None, :] * jnp.sin(angles)
    return jnp.stack([real_rows, imag_rows], axis=1).reshape(2 * K, NT).astype(jnp.bfloat16)


def transform(piece):
    snap_total, item_count, cell_count = piece.shape
    blocks = piece.reshape(NB, NT, item_count * cell_count)
    spectra = jnp.einsum(
        "jn,bnc->jbc", spectral_table(), blocks, preferred_element_type=jnp.float32
    )
    return spectra.astype(jnp.bfloat16).reshape(K, 2, NB, item_count, cell_count)


def triad_terms(spectra, weight_rows, triads, triad_index):
    count = triad_index.shape[0]
    lane_total = weight_rows.shape[0]
    triad_freqs = jnp.take(triads, triad_index, axis=0)
    first_spec = (
        jnp.take(spectra, triad_freqs[:, 0], axis=0)
        .reshape(count, 2, NB, lane_total)
        .astype(jnp.float32)
    )
    second_spec = (
        jnp.take(spectra, triad_freqs[:, 1], axis=0)
        .reshape(count, 2, NB, lane_total)
        .astype(jnp.float32)
    )
    third_spec = jnp.take(spectra, triad_freqs[:, 2], axis=0).reshape(count, 2, NB, lane_total)
    prod_real = (
        first_spec[:, 0] * second_spec[:, 0] - first_spec[:, 1] * second_spec[:, 1]
    ) * weight_rows
    prod_imag = (
        first_spec[:, 0] * second_spec[:, 1] + first_spec[:, 1] * second_spec[:, 0]
    ) * weight_rows
    product = jnp.stack([prod_real, prod_imag], axis=1).astype(jnp.bfloat16)
    gram = jnp.einsum("trbc,tsdc->trbsd", product, third_spec, preferred_element_type=jnp.float32)
    bis_real = gram[:, 0, :, 0, :] + gram[:, 1, :, 1, :]
    bis_imag = gram[:, 0, :, 1, :] - gram[:, 1, :, 0, :]
    return jnp.stack([bis_real, bis_imag], axis=1).reshape(count, 2 * NB * NB)


def block_size(amount, quantum):
    return quantum * math.gcd(amount // quantum, max(1, 64 // quantum))


def blocked(index_list, quantum, spectra, weight_rows, triads):
    amount = index_list.shape[0]
    width_blk = block_size(amount, quantum)
    grouped = index_list.reshape(amount // width_blk, width_blk)

    def group_terms(slot_group):
        filled = (slot_group >= 0).astype(jnp.float32)
        return (
            triad_terms(spectra, weight_rows, triads, jnp.maximum(slot_group, 0)) * filled[:, None]
        )

    return lax.map(group_terms, grouped).reshape(amount, 2 * NB * NB)


def shards(snapshots, cell_weights, triads, owner_slots):
    spectra = transform(lax.all_to_all(snapshots, "tm", split_axis=2, concat_axis=0, tiled=True))
    cell_count = spectra.shape[4]
    spectra = spectra.reshape(K, 2 * NB * 3 * cell_count)
    tm_total = lax.axis_size("tm")
    space_total = lax.axis_size("space")
    device_total = tm_total * space_total
    weight_scale = 1.0 / math.sqrt(3.0 * cell_count * device_total)
    local_w = (
        lax.dynamic_slice_in_dim(cell_weights, lax.axis_index("tm") * cell_count, cell_count, 0)
        * weight_scale
    )
    weight_rows = jnp.tile(local_w, 3)
    flat_slots = owner_slots.reshape(-1)
    my_rows = flat_slots.shape[0] // device_total
    return lax.psum_scatter(
        blocked(flat_slots, my_rows, spectra, weight_rows, triads),
        ("tm", "space"),
        scatter_dimension=0,
        tiled=True,
    )


def solution(mesh):
    placed = (P("tm", None, "space"), P("space"), P(), P())
    return jax.shard_map(
        shards, mesh=mesh, in_specs=placed, out_specs=P(("tm", "space"), None), check_vma=False
    )
```

profile of v0, /device:TPU:0, one launch (start us, length us, event | category | flops | bytes accessed | tf_op | source)
XLA Modules:
  0.0 327.5 jit_solution(2348501136595664732)
XLA Ops:
  6.5 7.7 %copy.36 = bf16[512,3,1024]{0,1,2:T(4,128)(2,1)} copy(bf16[512,3,1024]{2,0,1:T(8,128)(2,1)} %param.8) | data formatting | bytes 6291456 | tf_op args[0]
  14.2 7.4 %all-to-all-start = ((bf16[512,3,1024]{0,1,2:T(4,128)(2,1)}), bf16[512,3,1024]{0,1,2:T(4,128)(2,1)}, u32[]{:S(2)}, u32[]{:S(2)}) async-start(bf16[512,3,1024]{0,1,2:T(4,128)(2,1)} %copy.36), calls=%async_computation | async-start | bytes 8388608 | tf_op jit(solution)/shard_map/all_to_all | solution.py:80
  22.7 0.8 dynamic-slice_multiply_fusion
  23.5 91.4 %all-to-all-done = bf16[512,3,1024]{0,1,2:T(4,128)(2,1)} async-done(((bf16[512,3,1024]{0,1,2:T(4,128)(2,1)}), bf16[512,3,1024]{0,1,2:T(4,128)(2,1)}, u32[]{:S(2)}, u32[]{:S(2)}) %all-to-all-start) | async-done | bytes 3145760 | tf_op jit(solution)/shard_map/all_to_all | solution.py:80
  114.9 4.5 %copy.54 = bf16[512,3,8,128]{0,2,3,1:T(8,128)(2,1)S(1)} copy(bf16[512,3,8,128]{0,1,3,2:T(4,128)(2,1)} %bitcast) | data formatting | bytes 6291456 | tf_op jit(solution)/shard_map/all_to_all | solution.py:80
  119.4 3.4 %reshape.253 = bf16[16,256,384]{1,0,2:T(8,128)(2,1)} reshape(bf16[8,512,3,128]{1,0,3,2:T(8,128)(2,1)S(1)} %bitcast.74) | data formatting | bytes 6291456 | tf_op jit(solution)/shard_map/reshape | solution.py:26
  122.7 4.2 %fusion.12 = bf16[256,16,384]{2,0,1:T(8,128)(2,1)S(1)} fusion(bf16[256,256,1]{1,0,2:T(8,128)(2,1)S(1)} %reshape.310, bf16[16,256,384]{1,0,2:T(8,128)(2,1)} %reshape.253), kind=kOutput, calls=%fused_computation.46 | convolution fusion | flops 806879232 | bytes 6422528 | tf_op jit(solution)/shard_map/jn,bnc->jbc/dot_general | solution.py:27
  127.0 3.5 %copy.39 = bf16[256,16,384]{2,1,0:T(8,128)(2,1)} copy(bf16[256,16,384]{2,0,1:T(8,128)(2,1)S(1)} %fusion.12) | data formatting | bytes 6291456 | tf_op jit(solution)/shard_map/convert_element_type | solution.py:30
  130.5 4.2 %reshape_reshape.7 = bf16[128,12288]{1,0:T(8,128)(2,1)S(1)} reshape(bf16[256,16,384]{2,1,0:T(8,128)(2,1)} %copy.39) | data formatting | bytes 6291456 | tf_op jit(solution)/shard_map/reshape;reshape | solution.py:82
  134.7 60.4 %while.11 = (s32[]{:T(128)}, f32[2,64,512]{2,1,0:T(8,128)}, s32[2,64]{1,0:T(2,128)S(1)}, s32[64,3]{1,0:T(8,128)S(1)}, bf16[128,12288]{1,0:T(8,128)(2,1)S(1)}, /*index=5*/f32[128]{0:T(128)S(1)}, s32[]{:T(128)}) while((s32[]{:T(128)}, f32[2,64,512]{2,1,0:T(8,128)}, s32[2,64]{1,0:T(2,128)S(1)}, s32[64,3]{1,0:T(8,128)S(1)}, ...), condition=%wide.region_1.3_spmd.clone, body=%wide.region_0.2_spmd.clone.sunk | while | flops 61446336 | bytes 69630632 | solution.py:76
  134.7 0.6 gather_fusion
  135.7 2.7 gather_fusion.1
  138.4 1.7 select_convert_fusion.4
  140.0 2.2 copy.61
  142.3 2.7 gather_fusion.2
  145.0 1.7 select_convert_fusion.5
  146.7 0.6 copy.62
  147.2 1.3 copy-done
  148.5 1.7 multiply_convert_fusion.5
  150.2 2.7 gather_fusion.3
  152.9 1.6 broadcast_select_fusion.5
  154.8 0.9 copy-done.1
  155.9 2.9 fusion.30
  158.9 1.1 fusion.31
  160.0 1.3 copy.64
  161.3 1.3 copy.65
  162.6 0.8 copy.66
  163.4 1.6 constant_dynamic-update-slice_fusion.2
  164.9 0.6 gather_fusion
  165.9 2.7 gather_fusion.1
  168.6 1.7 select_convert_fusion.4
  170.2 2.2 copy.61
  172.5 2.7 gather_fusion.2
  175.2 1.7 select_convert_fusion.5
  176.9 0.6 copy.62
  177.4 1.3 copy-done
  178.7 1.7 multiply_convert_fusion.5
  180.4 2.7 gather_fusion.3
  183.1 1.6 broadcast_select_fusion.5
  185.0 0.9 copy-done.1
  186.1 2.9 fusion.30
  189.1 1.1 fusion.31
  190.2 1.3 copy.64
  191.5 1.3 copy.65
  192.8 0.8 copy.66
  193.6 1.6 constant_dynamic-update-slice_fusion.2
  195.1 124.2 %all-reduce.3.cloned.1.call-done = f32[128,512]{1,0:T(8,128)} async-done(((f32[128,512]{1,0:T(8,128)}), f32[128,512]{1,0:T(8,128)}) %all-reduce.3.cloned.1.call-update) | async-done | bytes 262160
  319.4 1.3 constant_dynamic-slice_fusion.1
  (55 shorter events, 2.9 us)
Async XLA Ops:
  14.2 8.4 %copy-start.4 = (s32[64,3]{0,1:T(4,128)S(1)}, s32[64,3]{0,1:T(4,128)}, u32[]{:S(2)}) copy-start(s32[64,3]{0,1:T(4,128)} %param.10) | copy-start | bytes 2308
  14.2 8.5 %copy-start.3 = (s32[8,16]{1,0:T(8,128)S(1)}, s32[8,16]{1,0:T(8,128)}, u32[]{:S(2)}) copy-start(s32[8,16]{1,0:T(8,128)} %param.11) | copy-start | bytes 1540
  14.2 100.7 %all-to-all-start = ((bf16[512,3,1024]{0,1,2:T(4,128)(2,1)}), bf16[512,3,1024]{0,1,2:T(4,128)(2,1)}, u32[]{:S(2)}, u32[]{:S(2)}) async-start(bf16[512,3,1024]{0,1,2:T(4,128)(2,1)} %copy.36), calls=%async_computation | async-start | bytes 8388608 | tf_op jit(solution)/shard_map/all_to_all | solution.py:80
  21.6 297.7 %all-reduce.3.cloned.1.call-start = ((), (), s32[]{:S(2)}) async-start(), calls=%async_computation.1 | async-start | bytes 524288
  146.6 1.9 copy-start
  154.5 1.1 copy-start.1
  154.5 1.4 copy-start.2
  176.8 1.9 copy-start
  184.7 1.1 copy-start.1
  184.8 1.4 copy-start.2
Sparse Core Ops, SparseCore 0:
  195.3 124.0 all-reduce.2
where the time goes:
time: 329 us; the launch traced here: 328 us
  waiting for transfers between devices  216 us (66%)
  local copies, waits for them, and re-layouts  63.2 us (19%)
  other arithmetic  17.4 us (5%)
  between operations  13.5 us (4%)
  matrix products  10.1 us (3%)
  starting transfers between devices  7.45 us (2%)
    unnamed x2, waiting for transfers between devices  124 us
    all_to_all x1, waiting for transfers between devices, shards(): lax.all_to_all(snapshots, 'tm', split_axis=2, concat_axis=0, tiled=True)  91.4 us
    while x18, local copies, waits for them, and re-layouts  10.8 us
    unnamed x7, local copies, waits for them, and re-layouts  9.08 us
    all_to_all x1, starting transfers between devices, shards(): lax.all_to_all(snapshots, 'tm', split_axis=2, concat_axis=0, tiled=True)  7.41 us
  transfers between devices with their start and end apart: 2, of which 2 were waited for; matrix products, arithmetic and copies ran while one was open for 1% of the time, Pallas kernels for 0%

commit v1 on v0

--- a/solution.py
+++ b/solution.py
@@ -77,7 +77,14 @@
 
 
 def shards(snapshots, cell_weights, triads, owner_slots):
-    spectra = transform(lax.all_to_all(snapshots, "tm", split_axis=2, concat_axis=0, tiled=True))
+    spectra = transform(
+        jnp.concatenate(
+            lax.all_to_all(
+                jnp.stack(jnp.split(snapshots, lax.axis_size("tm"), axis=2)), "tm", 0, 0
+            ),
+            axis=0,
+        )
+    )
     cell_count = spectra.shape[4]
     spectra = spectra.reshape(K, 2 * NB * 3 * cell_count)
     tm_total = lax.axis_size("tm")

time: 329 us -> 312 us (0.948)
  waiting for transfers between devices: 216 us -> 193 us
  local copies, waits for them, and re-layouts: 63.2 us -> 72.1 us
    all_to_all x1, waiting for transfers between devices: 91.4 us -> 68.8 us  [shards(): lax.all_to_all(jnp.stack(jnp.split(snapshots, lax.axis_size('tm'), axis=2...]
    another operation x0 -> x3, local copies, waits for them, and re-layouts: none -> 14.1 us  [the longest x2 12.3 us: transform(): blocks = piece.reshape(NB, NT, item_count * cell_count)]
    unnamed x7 -> x13, local copies, waits for them, and re-layouts: 9.08 us -> 13.9 us
    all_to_all x1 -> x0, local copies, waits for them, and re-layouts: 4.48 us -> none  [shards(): lax.all_to_all(snapshots, 'tm', split_axis=2, concat_axis=0, tiled=True)]
    reshape x1 -> x0, local copies, waits for them, and re-layouts: 3.36 us -> none  [transform(): blocks = piece.reshape(NB, NT, item_count * cell_count)]
where the time goes in v1:
time: 312 us; the launch traced here: 311 us
  waiting for transfers between devices  193 us (62%)
  local copies, waits for them, and re-layouts  72.1 us (23%)
  other arithmetic  17.6 us (6%)
  between operations  13.5 us (4%)
  starting transfers between devices  7.45 us (2%)
  matrix products  6.88 us (2%)
    unnamed x2, waiting for transfers between devices  124 us
    all_to_all x1, waiting for transfers between devices, shards(): lax.all_to_all(jnp.stack(jnp.split(snapshots, lax.axis_size('tm'), axis=2...  68.8 us
    unnamed x13, local copies, waits for them, and re-layouts  13.9 us
    another operation x2, local copies, waits for them, and re-layouts, transform(): blocks = piece.reshape(NB, NT, item_count * cell_count)  12.3 us
    while x18, local copies, waits for them, and re-layouts  8.67 us
    all_to_all x1, starting transfers between devices, shards(): lax.all_to_all(jnp.stack(jnp.split(snapshots, lax.axis_size('tm'), axis=2...  7.41 us
  transfers between devices with their start and end apart: 2, of which 2 were waited for; matrix products, arithmetic and copies ran while one was open for 1% of the time, Pallas kernels for 0%

profile of v1, /device:TPU:0, one launch (start us, length us, event | category | flops | bytes accessed | tf_op | source)
XLA Modules:
  0.0 310.8 jit_solution(11059580950329876665)
XLA Ops:
  6.5 1.8 bitcast_dynamic-update-slice_fusion.7
  8.3 1.8 bitcast_dynamic-update-slice_fusion.6
  10.1 1.8 bitcast_dynamic-update-slice_fusion.5
  11.9 1.8 bitcast_dynamic-update-slice_fusion.4
  13.7 1.8 bitcast_dynamic-update-slice_fusion.3
  15.4 1.8 bitcast_dynamic-update-slice_fusion.2
  17.2 1.8 bitcast_dynamic-update-slice_fusion.1
  19.0 1.8 bitcast_dynamic-update-slice_fusion
  20.8 7.4 %all-to-all-start = ((bf16[8,512,3,128]{3,1,2,0:T(8,128)(2,1)}), bf16[8,512,3,128]{3,1,2,0:T(8,128)(2,1)S(1)}, u32[]{:S(2)}, u32[]{:S(2)}) async-start(bf16[8,512,3,128]{3,1,2,0:T(8,128)(2,1)} %bitcast_dynamic-update-slice_fusion), calls=%async_computation | async-start | bytes 6291456 | tf_op jit(solution)/shard_map/all_to_all | solution.py:82
  30.1 68.8 %all-to-all-done = bf16[8,512,3,128]{3,1,2,0:T(8,128)(2,1)S(1)} async-done(((bf16[8,512,3,128]{3,1,2,0:T(8,128)(2,1)}), bf16[8,512,3,128]{3,1,2,0:T(8,128)(2,1)S(1)}, u32[]{:S(2)}, u32[]{:S(2)}) %all-to-all-start) | async-done | bytes 3145760 | tf_op jit(solution)/shard_map/all_to_all | solution.py:82
  98.9 4.6 %copy.41 = bf16[8,512,3,128]{3,2,1,0:T(4,128)(2,1)} copy(bf16[8,512,3,128]{3,1,2,0:T(8,128)(2,1)S(1)} %all-to-all-done) | data formatting | bytes 6291456 | tf_op jit(solution)/shard_map/reshape;reshape | solution.py:26
  103.6 7.7 %reshape.307 = bf16[16,256,384]{2,1,0:T(8,128)(2,1)S(1)} reshape(bf16[8,512,3,128]{3,2,1,0:T(4,128)(2,1)} %copy.41) | data formatting | bytes 6291456 | tf_op jit(solution)/shard_map/reshape;reshape | solution.py:26
  111.2 1.0 convolution_convert_fusion
  112.2 3.5 %copy.36 = bf16[256,16,384]{2,1,0:T(8,128)(2,1)} copy(bf16[256,16,384]{2,0,1:T(8,128)(2,1)S(1)} %convolution_convert_fusion) | data formatting | bytes 6291456 | tf_op jit(solution)/shard_map/convert_element_type | solution.py:30
  115.7 4.2 %reshape_reshape.11 = bf16[128,12288]{1,0:T(8,128)(2,1)S(1)} reshape(bf16[256,16,384]{2,1,0:T(8,128)(2,1)} %copy.36) | data formatting | bytes 6291456 | tf_op jit(solution)/shard_map/reshape;reshape | solution.py:89
  119.9 58.5 %while.11 = (s32[]{:T(128)}, f32[2,64,512]{2,1,0:T(8,128)}, s32[2,64]{1,0:T(2,128)S(1)}, s32[64,3]{1,0:T(8,128)S(1)}, bf16[128,12288]{1,0:T(8,128)(2,1)S(1)}, /*index=5*/f32[128]{0:T(128)S(1)}, s32[]{:T(128)}) while((s32[]{:T(128)}, f32[2,64,512]{2,1,0:T(8,128)}, s32[2,64]{1,0:T(2,128)S(1)}, s32[64,3]{1,0:T(8,128)S(1)}, ...), condition=%wide.region_1.3_spmd.clone, body=%wide.region_0.2_spmd.clone.sunk | while | flops 61446336 | bytes 69630632 | solution.py:76
  120.9 2.7 gather_fusion.1
  123.6 1.7 select_convert_fusion.4
  125.3 2.2 copy.54
  127.5 2.7 gather_fusion.2
  130.2 1.7 select_convert_fusion.5
  132.5 1.3 copy-done
  133.8 1.7 multiply_convert_fusion.5
  135.5 2.7 gather_fusion.3
  138.1 1.7 broadcast_select_fusion.5
  140.2 2.9 fusion.26
  143.1 1.1 fusion.27
  144.3 1.3 copy.57
  145.5 1.3 copy.58
  146.9 0.8 copy.59
  147.6 1.6 constant_dynamic-update-slice_fusion.2
  150.1 2.7 gather_fusion.1
  152.8 1.7 select_convert_fusion.4
  154.5 2.2 copy.54
  156.7 2.7 gather_fusion.2
  159.4 1.7 select_convert_fusion.5
  161.7 1.3 copy-done
  163.0 1.7 multiply_convert_fusion.5
  164.7 2.7 gather_fusion.3
  167.4 1.7 broadcast_select_fusion.5
  169.4 3.0 fusion.26
  172.4 1.1 fusion.27
  173.5 1.3 copy.57
  174.8 1.3 copy.58
  176.1 0.8 copy.59
  176.9 1.6 constant_dynamic-update-slice_fusion.2
  178.5 124.2 %all-reduce.3.cloned.1.call-done = f32[128,512]{1,0:T(8,128)} async-done(((f32[128,512]{1,0:T(8,128)}), f32[128,512]{1,0:T(8,128)}) %all-reduce.3.cloned.1.call-update) | async-done | bytes 262160
  302.6 1.3 constant_dynamic-slice_fusion.1
  (62 shorter events, 5.5 us)
Async XLA Ops:
  20.8 8.4 %copy-start.4 = (s32[64,3]{0,1:T(4,128)S(1)}, s32[64,3]{0,1:T(4,128)}, u32[]{:S(2)}) copy-start(s32[64,3]{0,1:T(4,128)} %param.10) | copy-start | bytes 2308
  20.8 8.5 %copy-start.3 = (s32[8,16]{1,0:T(8,128)S(1)}, s32[8,16]{1,0:T(8,128)}, u32[]{:S(2)}) copy-start(s32[8,16]{1,0:T(8,128)} %param.11) | copy-start | bytes 1540
  20.8 78.1 %all-to-all-start = ((bf16[8,512,3,128]{3,1,2,0:T(8,128)(2,1)}), bf16[8,512,3,128]{3,1,2,0:T(8,128)(2,1)S(1)}, u32[]{:S(2)}, u32[]{:S(2)}) async-start(bf16[8,512,3,128]{3,1,2,0:T(8,128)(2,1)} %bitcast_dynamic-update-slice_fusion), calls=%async_computation | async-start | bytes 6291456 | tf_op jit(solution)/shard_map/all_to_all | solution.py:82
  28.2 274.4 %all-reduce.3.cloned.1.call-start = ((), (), s32[]{:S(2)}) async-start(), calls=%async_computation.1 | async-start | bytes 524288
  131.9 1.9 copy-start
  138.1 2.0 copy-start.1
  138.1 2.0 copy-start.2
  161.1 1.9 copy-start
  167.4 2.0 copy-start.1
  167.4 2.0 copy-start.2
Sparse Core Ops, SparseCore 0:
  178.6 124.0 all-reduce.2
